TPU v7x, 256 devices: a whole 4x4x8 slice. The times are simulated.
256 devices in a mesh: band: 16 (over y_hi, z), comp: 16 (over y_lo, x, core).
Axes of the slice: x: 4, y: 4 (y_hi: 2, y_lo: 2; y = y_hi * 2 + y_lo), z: 8, core: 2. Of those that a mesh axis runs over, the one named last changes fastest.
Arguments:
- pair_dens: bfloat16 [6144, 8192], P('band', 'comp'), may hold values from -0.29882812 to 0.29882812
- pair_index: int32 [6144], P('band'), may hold values from 0 to 6143, each once
- val_energy: float32 [24], replicated, may hold values from -9 to -1
- cond_energy: float32 [256], replicated, may hold values from 0.5 to 12
- coul_root: float32 [8192], replicated, may hold values from 0.5 to 2
Outputs:
- epsilon: float32 [8192, 8192], P('band', 'comp')
- panel_factor: float32 [8192, 128], P(('band', 'comp'))
Inputs may be any that keep to these rules, and one draw needn't show every extreme that they name: `pair_index`: every pair number appears exactly once; pair number n joins valence band n // 256 with conduction band n % 256.
All inputs are finite; a program needn't handle non-finite values.
Results may differ from a plain program's by a relative error of at most 0.0022.
Values may be sent and summed in bfloat16 or wider, within the bound.
A program may use at most 64 MiB of HBM per device.

v0:
```python
import jax
import jax.numpy as jnp
from jax import lax
from jax.sharding import PartitionSpec as P

VAL = 24
COND = 256
PANEL = 128


def broadcast(value, axis, source):
    kept = jnp.where(lax.axis_index(axis) == source, value, 0).astype(value.dtype)
    return lax.psum(kept, axis)


def pair_weights(index, val_energy, cond_energy):
    valence = index // COND
    conduction = index % COND
    val_hot = valence[:, None] == jnp.arange(VAL, dtype=jnp.int32)[None, :]
    cond_hot = conduction[:, None] == jnp.arange(COND, dtype=jnp.int32)[None, :]
    low = jnp.sum(jnp.where(val_hot, val_energy[None, :], 0.0), axis=1)
    high = jnp.sum(jnp.where(cond_hot, cond_energy[None, :], 0.0), axis=1)
    return 4.0 / (high - low)


def shards(pair_dens, pair_index, val_energy, cond_energy, coul_root):
    col_width = pair_dens.shape[1]
    whole = lax.all_gather(pair_dens, "comp", axis=1, tiled=True)
    row_width = whole.shape[1] // lax.axis_size("band")
    contract = (((0,), (0,)), ((), ()))
    weight = pair_weights(pair_index, val_energy, cond_energy)
    scaled = (weight[:, None] * pair_dens.astype(jnp.float32)).astype(jnp.bfloat16)
    chi = lax.psum_scatter(
        lax.dot_general(whole, scaled, contract, preferred_element_type=jnp.float32),
        "band",
        scatter_dimension=0,
        tiled=True,
    )
    row_start = lax.axis_index("band") * row_width
    col_start = lax.axis_index("comp") * col_width
    row_root = lax.dynamic_slice_in_dim(coul_root, row_start, row_width, 0)
    col_root = lax.dynamic_slice_in_dim(coul_root, col_start, col_width, 0)
    row_ids = row_start + jnp.arange(row_width, dtype=jnp.int32)
    col_ids = col_start + jnp.arange(col_width, dtype=jnp.int32)
    unit = jnp.where(row_ids[:, None] == col_ids[None, :], 1.0, 0.0).astype(jnp.float32)
    epsilon = row_root[:, None] * chi * col_root[None, :] + unit
    leading = broadcast(epsilon[:, :PANEL], "comp", 0)
    block = broadcast(leading[:PANEL], "band", 0)
    lower = jnp.linalg.cholesky(block)
    sub_rows = row_width // lax.axis_size("comp")
    own_rows = lax.dynamic_slice_in_dim(leading, lax.axis_index("comp") * sub_rows, sub_rows, 0)
    panel_factor = jax.scipy.linalg.solve_triangular(lower, own_rows.T, lower=True).T
    return (epsilon, panel_factor)


def solution(mesh):
    in_specs = (P("band", "comp"), P("band"), P(), P(), P())
    out_specs = (P("band", "comp"), P(("band", "comp"), None))
    return jax.shard_map(shards, mesh=mesh, in_specs=in_specs, out_specs=out_specs, check_vma=False)
```

profile of v0, /device:TPU:2, one launch (start us, length us, event | category | flops | bytes accessed | tf_op | source)
XLA Modules:
  0.0 657.3 jit_solution(5992974143471621830)
XLA Ops:
  7.2 0.0 all-gather.2.cloned.1.call-start
  7.2 0.7 all-gather.2.cloned.1.call-update
  7.9 0.0 reduce-scatter.2.cloned.1.call-start
  7.9 0.7 add_select_fusion
  8.6 0.7 select_reduce_fusion.2
  9.4 0.9 select_reduce_fusion
  10.3 47.2 %all-gather.2.cloned.1.call-done = bf16[384,8192]{1,0:T(8,128)(2,1)} async-done(((bf16[384,512]{1,0:T(8,128)(2,1)}), bf16[384,8192]{1,0:T(8,128)(2,1)}) %all-gather.2.cloned.1.call-update) | async-done | bytes 6291472 | tf_op jit(solution)/shard_map/all_gather | solution.py:28
  57.5 13.2 %convolution_bitcast_fusion = f32[8192,512]{1,0:T(8,128)} fusion(bf16[384,8192]{1,0:T(8,128)(2,1)} %all-gather.2.cloned.1.call-done, bf16[384,512]{1,0:T(8,128)(2,1)} %param.5, f32[384]{0:T(512)S(1)} %subtract_divide_fusion), kind=kOutput, calls=%fused_computation | convolution fusion | flops 3221815296 | bytes 23463424 | tf_op jit(solution)/shard_map/dot_general | solution.py:34
  70.8 0.0 all-reduce.3.cloned.1.call-start
  70.8 0.8 fusion.8
  71.6 285.9 %reduce-scatter.2.cloned.1.call-done = f32[512,512]{1,0:T(8,128)} async-done(((f32[8192,512]{1,0:T(8,128)}), f32[512,512]{1,0:T(8,128)}) %reduce-scatter.2.cloned.1.call-update) | async-done | bytes 1048592 | tf_op jit(solution)/shard_map/reduce_scatter | solution.py:33
  357.6 1.5 select_add_fusion
  359.0 0.8 slice_select_fusion
  359.9 0.0 all-reduce.5.cloned.1.call-start
  360.0 115.8 %all-reduce.3.cloned.1.call-done = f32[512,128]{1,0:T(8,128)} async-done(((f32[512,128]{1,0:T(8,128)}), f32[512,128]{1,0:T(8,128)}) %all-reduce.3.cloned.1.call-update) | async-done | bytes 262160 | tf_op jit(solution)/shard_map/psum | solution.py:13
  475.7 1.5 slice_select_fusion.1
  477.2 147.4 %all-reduce.5.cloned.1.call-done = f32[128,128]{1,0:T(8,128)} async-done(((f32[128,128]{1,0:T(8,128)}), f32[128,128]{1,0:T(8,128)}) %all-reduce.5.cloned.1.call-update) | async-done | bytes 65552 | tf_op jit(solution)/shard_map/psum | solution.py:13
  624.6 0.9 copy.10
  625.5 0.9 fusion.4
  626.4 11.7 %cholesky.15 = f32[128,128]{1,0:T(8,128)S(1)} custom-call(f32[128,128]{1,0:T(8,128)S(1)} %fusion.4), custom_call_target="Cholesky" | custom-call | tf_op jit(solution)/shard_map/jit(cholesky)/cholesky | solution.py:49
  638.1 0.6 compare_reduce_fusion
  638.8 0.7 fusion.1
  639.4 9.8 %custom-call.7 = f32[1,128,128]{1,2,0:T(8,128)S(1)} custom-call(f32[1,128,128]{2,1,0:T(8,128)S(1)} %fusion.1), custom_call_target="InvertDiagBlocksLowerTriangular" | custom-call | tf_op jit(solution)/shard_map/jit(_solve_triangular)/triangular_solve | solution.py:52
  649.2 1.5 fusion.2
  (8 shorter events, 0.1 us)
Async XLA Ops:
  7.2 50.3 %all-gather.2.cloned.1.call-start = ((), (), s32[]{:S(2)}) async-start(), calls=%async_computation.1 | async-start | bytes 6684672 | tf_op jit(solution)/shard_map/all_gather | solution.py:28
  7.9 349.7 %reduce-scatter.2.cloned.1.call-start = ((), (), s32[]{:S(2)}) async-start(), calls=%async_computation.2 | async-start | bytes 17825792 | tf_op jit(solution)/shard_map/reduce_scatter | solution.py:33
  70.8 404.9 %all-reduce.3.cloned.1.call-start = ((), (), s32[]{:S(2)}) async-start(), calls=%async_computation.3 | async-start | bytes 524288 | tf_op jit(solution)/shard_map/psum | solution.py:13
  359.0 291.7 %copy-start = (f32[512,512]{1,0:T(8,128)}, f32[512,512]{1,0:T(8,128)S(1)}, u32[]{:S(2)}) copy-start(f32[512,512]{1,0:T(8,128)S(1)} %select_add_fusion) | copy-start | bytes 3145732
  359.9 264.7 %all-reduce.5.cloned.1.call-start = ((), (), s32[]{:S(2)}) async-start(), calls=%async_computation.4 | async-start | bytes 131072 | tf_op jit(solution)/shard_map/psum | solution.py:13
Sparse Core Ops, SparseCore 0:
  9.8 47.6 all-gather.1
  70.9 286.6 reduce-scatter.1
  360.2 115.4 all-reduce.2
  478.4 146.1 all-reduce.4
where the time goes:
time: 658 us; the launch traced here: 657 us
  waiting for transfers between devices  597 us (91%)
  other arithmetic  29.8 us (5%)
  matrix products  14.7 us (2%)
  between operations  13.8 us (2%)
    reduce_scatter x1, waiting for transfers between devices, shards(): lax.psum_scatter(lax.dot_general(whole, scaled, contract, preferred_eleme...  286 us
    psum x2, waiting for transfers between devices, broadcast(): return lax.psum(kept, axis)  263 us
    all_gather x1, waiting for transfers between devices, shards(): whole = lax.all_gather(pair_dens, 'comp', axis=1, tiled=True)  47.2 us
    dot_general x1, matrix products, shards(): lax.dot_general(whole, scaled, contract, preferred_element_type=jnp.float32)  13.2 us
  transfers between devices with their start and end apart: 4, of which 4 were waited for; matrix products, arithmetic and copies ran while one was open for 0% of the time, Pallas kernels for 0%

commit v1 on v0

v1 whole, which is shorter than its diff:
```python
import functools

import jax
import jax.numpy as jnp
from jax import lax
from jax.experimental import pallas as pl
from jax.experimental.pallas import tpu as pltpu
from jax.sharding import PartitionSpec as P

VAL = 24
COND = 256
PANEL = 128
MESH = pl.DeviceIdType.MESH

ROWS = 384
WIDTH = 512
NZ = 8
NC = 4
HS = WIDTH // NC
NP = WIDTH // PANEL
EARLY = 4
STEPS = 5
BLOCK = 16
ORDER = ((0, 0), (1, 0), (0, 1), (2, 0), (0, 2), (1, 1), (3, 0), (0, 3), (1, 2), (0, 4),
         (2, 1), (1, 3), (3, 1), (2, 2), (1, 4), (3, 2), (2, 3), (3, 3), (2, 4), (3, 4))
SUMS = ((0, 0), (1, 0), (0, 1), (2, 0), (3, 0), (0, 2), (1, 1), (0, 3), (1, 2), (0, 4),
        (1, 3), (1, 4), (2, 1), (3, 1), (2, 2), (3, 2), (2, 3), (3, 3), (2, 4), (3, 4))
LAG = 15
START = 12
RING = 2


def device(yl, x, k, yh, z):
    return (yh * NZ + z, yl * 8 + x * 2 + k)


def crossed(d):
    return jnp.logical_and(d >= 1, d <= 4)


def kernel(dens_in, index_in, val_in, cond_in, root_in, out, panel,
           dens, index, val_energy, cond_energy, root, in_sem, it, st, w, acc, sendb, recvb, outb, half, other, both_sides, prows, pmine,
           j_send, j_recv, w_send, w_recv, i_recv, x_send, y_send, s_send,
           p_send, p_recv, o_sem, a_sem, f_send, f_recv):
    b = lax.axis_index("band")
    c = lax.axis_index("comp")
    yh, z = b // NZ, b % NZ
    yl, x, k = c // 8, (c // 2) % 4, c % 2
    x0, k0 = z // 2, z % 2
    xr = (x - x0 + 4) % 4
    source_chip = xr == 0
    source = jnp.logical_and(source_chip, k == k0)

    up = device(yl, x, k, yh, (z + 1) % NZ)
    down = device(yl, x, k, yh, (z + NZ - 1) % NZ)
    xp = (x + 1) % 4
    xm = (x + 3) % 4
    sibling = device(yl, x, 1 - k, yh, z)
    far = device(yl, x, k, 1 - yh, z)

    load_dens = pltpu.make_async_copy(dens_in, dens, in_sem.at[0])
    load_root = pltpu.make_async_copy(root_in, root, in_sem.at[1])
    loads = (pltpu.make_async_copy(index_in, index, in_sem.at[2]),
             pltpu.make_async_copy(val_in, val_energy, in_sem.at[3]),
             pltpu.make_async_copy(cond_in, cond_energy, in_sem.at[4]),
             load_root)
    load_dens.start()
    for load in loads:
        load.start()
    barrier = pltpu.get_barrier_semaphore()
    partners = [up, down, sibling, far]
    for core in (0, 1):
        partners.append(device(yl, xp, core, yh, z))
        partners.append(device(yl, xm, core, yh, z))
        partners.append(device(1 - yl, x, core, yh, z))
    for partner in partners:
        pl.semaphore_signal(barrier, inc=1, device_id=partner, device_id_type=MESH)

    load_dens.wait()
    for n in range(NC):
        it[RING, 0, n] = dens[:, n * HS:(n + 1) * HS].T

    lead = c == 0

    def column(i):
        return (b, i)

    @pl.when(lead)
    def _():
        for i in range(1, 16):
            pl.semaphore_signal(barrier, inc=1, device_id=column(i), device_id_type=MESH)

    @pl.when(c != 0)
    def _():
        pl.semaphore_signal(barrier, inc=1, device_id=column(0), device_id_type=MESH)

    pl.semaphore_wait(barrier, len(partners) + jnp.where(lead, 15, 1))

    def j_copy(n, d, target):
        later = d + 1 if target is down else (d + NZ - 1) % NZ
        return pltpu.make_async_remote_copy(
            it.at[RING, d, n], it.at[RING, later, n], j_send.at[n, later], j_recv.at[n, later],
            device_id=target, device_id_type=MESH)

    def j_wait(n, d):
        pltpu.make_async_remote_copy(
            it.at[RING, d, n], it.at[RING, d, n], j_send.at[n, d], j_recv.at[n, d],
            device_id=up, device_id_type=MESH).wait_recv()

    def w_copy(d, target):
        later = d + 1 if target is down else (d + NZ - 1) % NZ
        return pltpu.make_async_remote_copy(
            w.at[d], w.at[later], w_send.at[later], w_recv.at[later],
            device_id=target, device_id_type=MESH)

    def w_wait(d):
        pltpu.make_async_remote_copy(
            w.at[d], w.at[d], w_send.at[d], w_recv.at[d],
            device_id=up, device_id_type=MESH).wait_recv()

    def own_sends(n):
        j_copy(n, 0, down).start()
        j_copy(n, 0, up).start()

    def i_copy(src, blk, n, d, send, target):
        return pltpu.make_async_remote_copy(
            src, it.at[blk, d, n], send, i_recv.at[blk, n, d],
            device_id=target, device_id_type=MESH)

    def i_wait(blk, n, d):
        i_copy(it.at[blk, d, n], blk, n, d, s_send.at[blk, n, d], sibling).wait_recv()

    def source_copies(n, d):
        src = it.at[RING, d, n]
        h = n % 2
        return [
            i_copy(src, yl, n, d, y_send.at[n, d], device(1 - yl, x, h, yh, z)),
            i_copy(src, yl, n, d, x_send.at[yl, n, d], device(yl, (x + 5 - 2 * h) % 4, h, yh, z)),
            i_copy(src, yl, n, d, s_send.at[yl, n, d], sibling),
        ]

    def source_sends(n, d):
        for copy in source_copies(n, d):
            copy.start()

    own_sends(0)
    own_sends(1)

    for load in loads:
        load.wait()
    number = jnp.broadcast_to(index[...].reshape(1, ROWS), (8, ROWS))
    valence = number // COND
    conduction = number % COND

    def pick(table, which, n):
        def body(i, kept):
            return jnp.where(which == i, table[i], kept)
        return lax.fori_loop(0, n, body, jnp.zeros((8, ROWS), jnp.float32), unroll=8)

    high = pick(cond_energy, conduction, COND)
    low = pick(val_energy, valence, VAL)
    w[0] = 4.0 / (high - low)
    w_copy(0, down).start()
    w_copy(0, up).start()

    hops = jnp.where(k == 0, xr, (4 - xr) % 4)
    lag_x = hops * 3
    lag_y = lag_x + 3
    lag_c = LAG
    forward_x = jnp.where(k == 0, jnp.logical_or(xr == 1, xr == 2), jnp.logical_or(xr == 3, xr == 2))
    x_target = device(yl, (x + 5 - 2 * k) % 4, k, yh, z)
    y_target = device(1 - yl, x, k, yh, z)

    def x_copy(blk, n, d):
        return i_copy(it.at[blk, d, n], blk, n, d, x_send.at[blk, n, d], x_target)

    def y_copy(n, d):
        return i_copy(it.at[yl, d, n], yl, n, d, y_send.at[n, d], y_target)

    def s_copy(blk, n, d):
        return i_copy(it.at[blk, d, n], blk, n, d, s_send.at[blk, n, d], sibling)

    def j_step(n, t):
        h = n % 2
        inner = jnp.logical_and(t >= 1, t <= 3)

        @pl.when(inner)
        def _():
            j_wait(n, t)

            @pl.when(jnp.logical_or(t < 3, h == 0))
            def _():
                j_copy(n, t, down).start()
            j_wait(n, NZ - t)

            @pl.when(jnp.logical_or(t < 3, h == 1))
            def _():
                j_copy(n, NZ - t, up).start()

            @pl.when(n == 0)
            def _():
                w_wait(t)
                w_wait(NZ - t)
                w_copy(t, down).start()

                @pl.when(t < 3)
                def _():
                    w_copy(NZ - t, up).start()

        @pl.when(t == 4)
        def _():
            j_wait(n, 4)

            @pl.when(n == 0)
            def _():
                w_wait(4)

        @pl.when(source)
        def _():
            source_sends(n, t)

            @pl.when(inner)
            def _():
                source_sends(n, NZ - t)

    def both(act):
        def run(n, t):
            act(n, t)

            @pl.when(jnp.logical_and(t >= 1, t <= 3))
            def _():
                act(n, NZ - t)
        return run

    def x_step(n, d):
        @pl.when(jnp.logical_and(n % 2 == k, jnp.logical_not(source_chip)))
        def _():
            i_wait(yl, n, d)

            @pl.when(forward_x)
            def _():
                x_copy(yl, n, d).start()

            @pl.when(jnp.logical_not(crossed(d)))
            def _():
                y_copy(n, d).start()
            s_copy(yl, n, d).start()

    def y_step(n, d):
        @pl.when(n % 2 == k)
        def _():
            i_wait(1 - yl, n, d)

            @pl.when(jnp.logical_and(crossed(d), jnp.logical_or(source_chip, forward_x)))
            def _():
                x_copy(1 - yl, n, d).start()
            s_copy(1 - yl, n, d).start()

    own_row = jnp.where(source, RING, yl)

    def compute_step(n, t):
        def arrived(d):
            @pl.when(jnp.logical_not(source))
            def _():
                @pl.when(jnp.logical_or(source_chip, n % 2 != k))
                def _():
                    i_wait(yl, n, d)

            @pl.when(n % 2 != k)
            def _():
                i_wait(1 - yl, n, d)

        both(lambda n, d: arrived(d))(n, t)
        def rows(d):
            return jnp.concatenate([it[own_row, d, n], it[1 - yl, d, n]], axis=0)

        def product(left, right):
            return lax.dot_general(left, right, (((1,), (1,)), ((), ())), preferred_element_type=jnp.float32)

        @pl.when(t == 0)
        def _():
            part = product(rows(0), st[0])
            acc[yl, n] = part[:HS]
            acc[1 - yl, n] = part[HS:]

        @pl.when(jnp.logical_and(t >= 1, t <= 3))
        def _():
            part = product(jnp.concatenate([rows(t), rows(NZ - t)], axis=1),
                           jnp.concatenate([st[t], st[NZ - t]], axis=1))
            acc[yl, n] += part[:HS]
            acc[1 - yl, n] += part[HS:]

        @pl.when(t == 4)
        def _():
            part = product(rows(4), st[4])
            acc[yl, n] += part[:HS]
            acc[1 - yl, n] += part[HS:]
            for p in range(NP):
                sendb[n, p] = acc[1 - yh, n, :, p * PANEL:(p + 1) * PANEL].astype(jnp.bfloat16)
            for p in range(EARLY):
                p_copy(n, p).start()

            @pl.when(n == 0)
            def _():
                for p in range(EARLY, NP):
                    p_copy(0, p).start()

            @pl.when(n == NC - 1)
            def _():
                for p in range(EARLY, NP):
                    for i in range(1, NC):
                        p_copy(i, p).start()

    def scale(n, d):
        wide = it[RING, d, n].astype(jnp.float32)
        st[d, pl.ds(n * HS, HS)] = (w[d, 0:1, :] * wide).astype(jnp.bfloat16)

    def p_copy(n, p):
        return pltpu.make_async_remote_copy(
            sendb.at[n, p], recvb.at[n, p], p_send.at[n, p], p_recv.at[n, p],
            device_id=far, device_id_type=MESH)

    def o_copy(n, p):
        return pltpu.make_async_copy(
            outb.at[n, p], out.at[pl.ds(n * HS, HS), pl.ds(p * PANEL, PANEL)], o_sem.at[n, p])

    def finish(n, p):
        p_copy(n, p).wait_recv()
        row = root[pl.ds(b * 4 + n, 1), :]
        rows = jnp.broadcast_to(row, (128, 128)).T
        row_ids = b * WIDTH + n * HS + lax.broadcasted_iota(jnp.int32, (HS, 128), 0)
        col = root[pl.ds(c * 4 + p, 1), :]
        col_ids = c * WIDTH + p * PANEL + lax.broadcasted_iota(jnp.int32, (HS, PANEL), 1)
        unit = jnp.where(row_ids == col_ids, 1.0, 0.0).astype(jnp.float32)
        total = acc[yh, n, :, p * PANEL:(p + 1) * PANEL] + recvb[n, p].astype(jnp.float32)
        outb[n, p] = rows * total * col + unit
        o_copy(n, p).start()

    last = STEPS * NC

    def pick_event(e, order):
        code = 0
        for i in range(0, len(order), 6):
            word = sum((t * NC + n) << (5 * j) for j, (n, t) in enumerate(order[i:i + 6]))
            code = jnp.where(e >= i, (word >> (e % 6 * 5)) & 31, code)
        return code & 3, code >> 2

    def events(e, act):
        @pl.when(jnp.logical_and(e >= 0, e < last))
        def _():
            act(*pick_event(e, ORDER))

    def computes(e):
        @pl.when(jnp.logical_and(e >= 0, e < last))
        def _():
            compute_step(*pick_event(e, SUMS))

    def a_copy():
        return pltpu.make_async_remote_copy(
            half, other, a_sem.at[0], a_sem.at[1], device_id=far, device_id_type=MESH)

    def lead_part(d):
        half[...] += lax.dot_general(it[RING, d, 0], st[d, 0:HS], (((1,), (1,)), ((), ())),
                                     preferred_element_type=jnp.float32)

    def first(n, t):
        j_step(n, t)
        both(scale)(n, t)

        @pl.when(jnp.logical_and(t == 0, n + 2 < NC))
        def _():
            own_sends(n + 2)

        @pl.when(jnp.logical_and(lead, n == 0))
        def _():
            both(lambda n, d: lead_part(d))(n, t)

            @pl.when(t == 4)
            def _():
                a_copy().start()

    lanes = lax.broadcasted_iota(jnp.int32, (BLOCK, PANEL), 1)
    subs = lax.broadcasted_iota(jnp.int32, (BLOCK, 1), 0)

    def factor_begin():
        a_copy().wait_recv()
        row = root[0:1, :]
        rows = jnp.broadcast_to(row, (PANEL, PANEL)).T
        ids = lax.broadcasted_iota(jnp.int32, (PANEL, PANEL), 0)
        unit = jnp.where(ids == lax.broadcasted_iota(jnp.int32, (PANEL, PANEL), 1), 1.0, 0.0)
        block = rows * (half[...] + other[...]) * row + unit
        both_sides[:, 0:PANEL] = (block + block.T) * 0.5
        both_sides[:, PANEL:] = unit

    def factor_block(j):
        base = pl.multiple_of(j * BLOCK, BLOCK)
        rows = both_sides[pl.ds(base, BLOCK), :]
        for i in range(BLOCK):
            col = jnp.sum(jnp.where(lanes == base + i, rows[:, 0:PANEL], 0.0), axis=1, keepdims=True)
            pivot = col[i:i + 1]
            inv = lax.rsqrt(pivot)
            inv = inv * (1.5 - 0.5 * pivot * inv * inv)
            line = rows[i:i + 1] * inv
            rows = jnp.where(subs > i, rows - (col * inv) * line, jnp.where(subs == i, line, rows))
        below = jnp.where(lanes >= base + BLOCK, rows[:, 0:PANEL], 0.0)
        both_sides[pl.ds(base, BLOCK), :] = rows
        both_sides[...] -= lax.dot_general(below, rows, (((0,), (0,)), ((), ())),
                                           precision=lax.Precision.HIGHEST,
                                           preferred_element_type=jnp.float32)

    def turn(e, carry):
        events(e, first)
        events(e - lag_x, both(x_step))
        events(e - lag_y, both(y_step))
        computes(e - lag_c)

        @pl.when(lead)
        def _():
            @pl.when(e == START)
            def _():
                factor_begin()

            @pl.when(jnp.logical_and(e >= START, e < START + PANEL // BLOCK))
            def _():
                factor_block(e - START)
        return carry

    @pl.when(lead)
    def _():
        half[...] = jnp.zeros_like(half)

    lax.fori_loop(0, last + LAG, turn, 0)

    def sent(n, carry):
        def each(d, inner):
            @pl.when(source)
            def _():
                for copy in source_copies(n, d):
                    copy.wait_send()

            @pl.when(n % 2 == k)
            def _():
                @pl.when(jnp.logical_not(source_chip))
                def _():
                    @pl.when(forward_x)
                    def _():
                        x_copy(yl, n, d).wait_send()

                    @pl.when(jnp.logical_not(crossed(d)))
                    def _():
                        y_copy(n, d).wait_send()
                    s_copy(yl, n, d).wait_send()

                @pl.when(jnp.logical_and(crossed(d), jnp.logical_or(source_chip, forward_x)))
                def _():
                    x_copy(1 - yl, n, d).wait_send()
                s_copy(1 - yl, n, d).wait_send()
            return inner
        lax.fori_loop(0, NZ, each, 0)
        for d in range(1, NZ):
            if d < 4:
                j_copy(n, d - 1, down).wait_send()
            elif d > 4:
                j_copy(n, (d + 1) % NZ, up).wait_send()
            else:
                j_copy(n, 3, down).wait_send()
        return carry

    lax.fori_loop(0, NC, sent, 0)
    for d in range(1, NZ):
        if d <= 4:
            w_copy(d - 1, down).wait_send()
        else:
            w_copy((d + 1) % NZ, up).wait_send()

    def f_copy(i):
        return pltpu.make_async_remote_copy(
            prows.at[i], pmine, f_send.at[i], f_recv.at[0], device_id=column(i), device_id_type=MESH)

    def f_out(src):
        return pltpu.make_async_copy(src, panel, f_recv.at[1])

    for n in range(NC):
        finish(n, 0)

        @pl.when(lead)
        def _():
            solved = lax.dot_general(outb[n, 0], both_sides[:, PANEL:], (((1,), (1,)), ((), ())),
                                     precision=lax.Precision.HIGHEST, preferred_element_type=jnp.float32)
            for i in range(4):
                prows[4 * n + i] = solved[32 * i:32 * (i + 1)]
                if n or i:
                    f_copy(4 * n + i).start()
                else:
                    f_out(prows.at[0]).start()

    for p in range(1, NP):
        for n in range(NC):
            finish(n, p)

    @pl.when(c != 0)
    def _():
        f_copy(1).wait_recv()
        f_out(pmine).start()
        f_out(pmine).wait()

    @pl.when(lead)
    def _():
        f_out(prows.at[0]).wait()
        a_copy().wait_send()
        for i in range(1, 16):
            f_copy(i).wait_send()

    for n in range(NC):
        for p in range(NP):
            p_copy(n, p).wait_send()
            o_copy(n, p).wait()


def epsilon_block(pair_dens, pair_index, val_energy, cond_energy, coul_root):
    hbm = pl.BlockSpec(memory_space=pltpu.HBM)
    dma = pltpu.SemaphoreType.DMA
    return pl.pallas_call(
        kernel,
        out_shape=(jax.ShapeDtypeStruct((WIDTH, WIDTH), jnp.float32),
                   jax.ShapeDtypeStruct((WIDTH // 16, PANEL), jnp.float32)),
        in_specs=[hbm] * 5,
        out_specs=(pl.BlockSpec(memory_space=pl.ANY), pl.BlockSpec(memory_space=pl.ANY)),
        scratch_shapes=[
            pltpu.VMEM((ROWS, WIDTH), jnp.bfloat16),
            pltpu.VMEM((ROWS,), jnp.int32),
            pltpu.SMEM((VAL,), jnp.float32),
            pltpu.SMEM((COND,), jnp.float32),
            pltpu.VMEM((64, 128), jnp.float32),
            dma((5,)),
            pltpu.VMEM((3, NZ, NC, HS, ROWS), jnp.bfloat16),
            pltpu.VMEM((NZ, WIDTH, ROWS), jnp.bfloat16),
            pltpu.VMEM((NZ, 8, ROWS), jnp.float32),
            pltpu.VMEM((2, NC, HS, WIDTH), jnp.float32),
            pltpu.VMEM((NC, NP, HS, PANEL), jnp.bfloat16),
            pltpu.VMEM((NC, NP, HS, PANEL), jnp.bfloat16),
            pltpu.VMEM((NC, NP, HS, PANEL), jnp.float32),
            pltpu.VMEM((PANEL, PANEL), jnp.float32),
            pltpu.VMEM((PANEL, PANEL), jnp.float32),
            pltpu.VMEM((PANEL, 2 * PANEL), jnp.float32),
            pltpu.VMEM((16, 32, PANEL), jnp.float32),
            pltpu.VMEM((32, PANEL), jnp.float32),
            dma((NC, NZ)), dma((NC, NZ)), dma((NZ,)), dma((NZ,)),
            dma((2, NC, NZ)), dma((2, NC, NZ)), dma((NC, NZ)), dma((2, NC, NZ)),
            dma((NC, NP)), dma((NC, NP)), dma((NC, NP)), dma((2,)), dma((16,)), dma((2,)),
        ],
        compiler_params=pltpu.CompilerParams(
            collective_id=0, has_side_effects=True, vmem_limit_bytes=60 * 1024 * 1024),
    )(pair_dens, pair_index, val_energy, cond_energy, coul_root.reshape(64, 128))


def shards(pair_dens, pair_index, val_energy, cond_energy, coul_root):
    return tuple(epsilon_block(pair_dens, pair_index, val_energy, cond_energy, coul_root))


def solution(mesh):
    in_specs = (P("band", "comp"), P("band"), P(), P(), P())
    out_specs = (P("band", "comp"), P(("band", "comp"), None))
    return jax.shard_map(shards, mesh=mesh, in_specs=in_specs, out_specs=out_specs, check_vma=False)
```

time: 658 us -> 82.8 us (0.13)
  waiting for transfers between devices: 597 us -> 0 us
  Pallas kernels: 0 us -> 77.7 us
  other arithmetic: 29.8 us -> 0 us
  matrix products: 14.7 us -> 0 us
  between operations: 13.8 us -> 0.65 us
    reduce_scatter x1 -> x0, waiting for transfers between devices: 286 us -> none  [shards(): lax.psum_scatter(lax.dot_general(whole, scaled, contract, preferred_eleme...]
    psum x2 -> x0, waiting for transfers between devices: 263 us -> none  [broadcast(): return lax.psum(kept, axis)]
    pallas_call x0 -> x1, Pallas kernels: none -> 77.7 us  [epsilon_block(): pl.pallas_call(kernel, out_shape=(jax.ShapeDtypeStruct((WIDTH, WIDTH), jn...]
    all_gather x1 -> x0, waiting for transfers between devices: 47.2 us -> none  [shards(): whole = lax.all_gather(pair_dens, 'comp', axis=1, tiled=True)]
    another operation x5 -> x0, other arithmetic: 22.9 us -> none  [the longest x3 12.4 us: shards(): lower = jnp.linalg.cholesky(block)]
    dot_general x1 -> x0, matrix products: 13.2 us -> none  [shards(): lax.dot_general(whole, scaled, contract, preferred_element_type=jnp.float32)]
  transfers between devices with their start and end apart: 4 -> 0, of which waited for: 4 -> 0; matrix products, arithmetic and copies ran while one was open for 0% -> 0% of each run, Pallas kernels for 0% -> 0%
where the time goes in v1:
time: 82.8 us; the launch traced here: 81.3 us
  Pallas kernels  77.7 us (94%)
  local copies, waits for them, and re-layouts  2.88 us (3%)
    pallas_call x1, Pallas kernels, epsilon_block(): pl.pallas_call(kernel, out_shape=(jax.ShapeDtypeStruct((WIDTH, WIDTH), jn...  77.7 us
    unnamed x4, local copies, waits for them, and re-layouts  2.88 us

profile of v1, /device:TPU:2, one launch (start us, length us, event | category | flops | bytes accessed | tf_op | source)
XLA Modules:
  0.0 81.3 jit_solution(7395258161484358552)
XLA Ops:
  0.6 77.7 %shard_map.68 = (f32[512,512]{1,0:T(8,128)}, f32[32,128]{1,0:T(8,128)}) custom-call(bf16[384,512]{1,0:T(8,128)(2,1)} %dens_in.1, s32[384]{0:T(512)} %index_in.1, f32[24]{0:T(128)} %val_in.1, f32[256]{0:T(256)} %cond_in.1, f32[64,128]{1,0:T(8,128)} %bitcast.1), custom_call_target="tpu_custom_call" | custom-call | tf_op jit(solution)/shard_map/pallas_call | solution.py:523
  78.4 0.0 copy-start
  78.4 2.3 %copy.9 = f32[512,512]{1,0:T(8,128)} copy(f32[512,512]{1,0:T(8,128)} %get-tuple-element.4) | data formatting | bytes 2097152
  80.6 0.0 copy-done
  80.6 0.6 copy.10
Async XLA Ops:
  78.4 2.3 %copy-start = (f32[32,128]{1,0:T(8,128)S(1)}, f32[32,128]{1,0:T(8,128)}, u32[]{:S(2)}) copy-start(f32[32,128]{1,0:T(8,128)} %get-tuple-element.5) | copy-start | bytes 49156
